TPU v7x, 32 devices: a whole 2x2x4 slice. The times are simulated.
32 devices in a mesh: dp: 4 (over z), node: 4 (over y, x), local: 2 (over core).
Axes of the slice: x: 2, y: 2, z: 4, core: 2. Of those that a mesh axis runs over, the one named last changes fastest.
Arguments:
- tokens: bfloat16 [128, 3584], P(('dp', 'node', 'local')), may hold values from -6 to 6
- routes: int32 [128, 2], P(('dp', 'node', 'local')), may hold values from 0 to 3, all different within a row; in each aligned block of 32 rows (0 to 31, 32 to 63, ...) at most 32 rows name the same one
- gate_fix: int32 [128, 2], P(('dp', 'node', 'local')), may hold values from 1 to 65535
- keep: int32 [128, 2], P(('dp', 'node', 'local')), may hold values 0 or 1
- seq_lengths: int32 [4, 2], P('dp'), may hold values from 1024 to 4096, as said below
- cotangent: bfloat16 [128, 3584], P(('dp', 'node', 'local')), may hold values from -6 to 6
- w_gate: bfloat16 [4, 1024, 3584], P('dp', ('node', 'local')), may hold values from -0.09375 to 0.09375
- w_up: bfloat16 [4, 1024, 3584], P('dp', ('node', 'local')), may hold values from -0.09375 to 0.09375
- w_down: bfloat16 [4, 1024, 3584], P('dp', ('node', 'local')), may hold values from -0.1875 to 0.1875
Outputs:
- layer_out: bfloat16 [128, 3584], P(('dp', 'node', 'local'))
- token_grad: bfloat16 [128, 3584], P(('dp', 'node', 'local'))
- grad_gate: bfloat16 [4, 1024, 3584], P('dp', ('node', 'local'))
- grad_down: bfloat16 [4, 1024, 3584], P('dp', ('node', 'local'))
Inputs may be any that keep to these rules, and one draw needn't show every extreme that they name: In each aligned block of 32 rows (the tokens of one group) no expert is named by more than 32 routes, a bound that some block reaches. `seq_lengths`: the chosen sequence of the first group counts all 4096 positions.
All inputs are finite; a program needn't handle non-finite values. No bound on the sum of `keep` on one device may be relied on, other than what follows from the above.
Results may differ from a plain program's by a relative error of at most 0.013.
Values may be sent and summed in bfloat16 or wider, within the bound.
A program may use at most 64 MiB of HBM per device.

v0:
```python
import jax
import jax.numpy as jnp
from jax import lax
from jax.sharding import PartitionSpec as P

SEQ = 4096


gate_unit = 1.0 / 65536.0


def slot_tables(route_ids, weight_fix, experts, shares, rank_count):
    tok_rows, topk = route_ids.shape
    flat_ids = route_ids.reshape(-1)
    onehot = (flat_ids[:, None] == jnp.arange(experts, dtype=jnp.int32)[None, :]).astype(jnp.int32)
    before = jnp.cumsum(onehot, axis=0) - onehot
    slot_index = jnp.sum(before * onehot, axis=1)
    target = slot_index // shares * (experts * shares) + flat_ids * shares + slot_index % shares
    places = jnp.arange(rank_count * experts * shares, dtype=jnp.int32)
    hit_table = (target[:, None] == places[None, :]).reshape(
        tok_rows, topk, rank_count * experts * shares
    )
    weight = (weight_fix.astype(jnp.float32) * gate_unit).reshape(tok_rows, topk, 1)
    select = jnp.any(hit_table, axis=1)
    combine = jnp.sum(jnp.where(hit_table, weight, jnp.float32(0.0)), axis=1)
    return (select, combine)


def token_scale(position, lengths, seq):
    seq_id = position // seq
    inside = position - seq_id * seq
    length = jnp.where(seq_id == 0, lengths[0], lengths[1])
    valid = (inside < length).astype(jnp.float32)
    sign = (1 - 2 * seq_id).astype(jnp.float32)
    return sign * valid * jnp.float32(seq) / length.astype(jnp.float32)


def send_back(rows_kept, experts, shares):
    model_width = rows_kept.shape[-1]
    return lax.all_to_all(
        rows_kept.reshape(experts, shares, model_width),
        "dp",
        split_axis=0,
        concat_axis=0,
        tiled=True,
    )


def settle(returned, table, my_rank, tok_rows):
    model_width = returned.shape[-1]
    gathered = lax.all_gather(returned[None], ("node", "local"), axis=0, tiled=True)
    own_rows = lax.dynamic_slice_in_dim(table, my_rank * tok_rows, tok_rows, 0)
    return jnp.dot(
        own_rows,
        gathered.reshape(-1, model_width).astype(jnp.float32),
        precision=lax.Precision.HIGHEST,
    ).astype(jnp.bfloat16)


def body(tokens, routes, gate_fix, keep, seq_lengths, cotangent, w_gate, w_up, w_down):
    tok_rows, model_width = tokens.shape
    topk = routes.shape[1]
    experts = lax.axis_size("dp")
    rank_count = lax.axis_size("node") * lax.axis_size("local")
    my_rank = lax.axis_index(("node", "local"))
    group_tok = tok_rows * rank_count
    shares = max(1, 2 * tok_rows * topk // experts)
    group_x, group_c = (
        lax.all_gather(tokens, ("node", "local"), axis=0, tiled=True),
        lax.all_gather(cotangent, ("node", "local"), axis=0, tiled=True),
    )
    group_r, group_w = (
        lax.all_gather(routes, ("node", "local"), axis=0, tiled=True),
        lax.all_gather(keep * gate_fix, ("node", "local"), axis=0, tiled=True),
    )
    select, combine = slot_tables(group_r, group_w, experts, shares, rank_count)
    span = 2 * SEQ // rank_count
    member = jnp.arange(group_tok, dtype=jnp.int32)
    position = member // tok_rows * span + member % tok_rows * (span // tok_rows)
    factor = token_scale(position, seq_lengths[0], SEQ)
    weighted = combine * factor[:, None]
    cot_float = group_c.astype(jnp.float32)
    buffer_x = jnp.dot(
        select.astype(jnp.bfloat16).T, group_x, preferred_element_type=jnp.float32
    ).astype(jnp.bfloat16)
    buffer_g = jnp.dot(weighted.T, cot_float, precision=lax.Precision.HIGHEST).astype(jnp.bfloat16)
    routed_x, routed_g = (
        lax.all_to_all(
            buffer_x.reshape(rank_count, experts, shares, model_width),
            "dp",
            split_axis=1,
            concat_axis=1,
            tiled=True,
        ),
        lax.all_to_all(
            buffer_g.reshape(rank_count, experts, shares, model_width),
            "dp",
            split_axis=1,
            concat_axis=1,
            tiled=True,
        ),
    )
    routed_x = routed_x.reshape(-1, model_width)
    routed_g = routed_g.reshape(-1, model_width)
    gate_slice = w_gate[0]
    up_slice = w_up[0]
    down_slice = w_down[0]
    gate_pre = jnp.einsum("sd,hd->sh", routed_x, gate_slice, preferred_element_type=jnp.float32)
    up_pre = jnp.einsum("sd,hd->sh", routed_x, up_slice, preferred_element_type=jnp.float32)
    sig_gate = jax.nn.sigmoid(gate_pre)
    silu_gate = gate_pre * sig_gate
    hidden = (silu_gate * up_pre).astype(jnp.bfloat16)
    out_rows = lax.psum_scatter(
        jnp.dot(hidden, down_slice, preferred_element_type=jnp.float32).astype(jnp.bfloat16),
        ("node", "local"),
        scatter_dimension=0,
        tiled=True,
    )
    back_out = send_back(out_rows, experts, shares)
    hidden_grad = jnp.einsum("sd,hd->sh", routed_g, down_slice, preferred_element_type=jnp.float32)
    dsilu = sig_gate * (1.0 + gate_pre * (1.0 - sig_gate))
    gate_delta = (hidden_grad * up_pre * dsilu).astype(jnp.bfloat16)
    up_delta = (hidden_grad * silu_gate).astype(jnp.bfloat16)
    grad_rows = lax.psum_scatter(
        (
            jnp.dot(gate_delta, gate_slice, preferred_element_type=jnp.float32)
            + jnp.dot(up_delta, up_slice, preferred_element_type=jnp.float32)
        ).astype(jnp.bfloat16),
        ("node", "local"),
        scatter_dimension=0,
        tiled=True,
    )
    back_grad = send_back(grad_rows, experts, shares)
    grad_gate = jnp.einsum(
        "sh,sd->hd", gate_delta, routed_x, preferred_element_type=jnp.float32
    ).astype(jnp.bfloat16)[None]
    grad_down = jnp.einsum(
        "sh,sd->hd", hidden, routed_g, preferred_element_type=jnp.float32
    ).astype(jnp.bfloat16)[None]
    layer_out = settle(back_out, combine, my_rank, tok_rows)
    token_grad = settle(back_grad, select.astype(jnp.float32), my_rank, tok_rows)
    return (layer_out, token_grad, grad_gate, grad_down)


def solution(mesh):
    in_specs = (
        P(("dp", "node", "local"), None),
        P(("dp", "node", "local"), None),
        P(("dp", "node", "local"), None),
        P(("dp", "node", "local"), None),
        P("dp", None),
        P(("dp", "node", "local"), None),
        P("dp", ("node", "local"), None),
        P("dp", ("node", "local"), None),
        P("dp", ("node", "local"), None),
    )
    out_specs = (
        P(("dp", "node", "local"), None),
        P(("dp", "node", "local"), None),
        P("dp", ("node", "local"), None),
        P("dp", ("node", "local"), None),
    )
    return jax.shard_map(body, mesh=mesh, in_specs=in_specs, out_specs=out_specs, check_vma=False)
```

profile of v0, /device:TPU:0, one launch (start us, length us, event | category | flops | bytes accessed | tf_op | source)
XLA Modules:
  0.0 215.1 jit_solution(17690074229721270404)
XLA Ops:
  7.2 10.6 %all-gather.2 = s32[8,4,2]{1,2,0:T(2,128)S(1)} all-gather(s32[1,4,2]{1,2,0:T(2,128)} %bitcast.48), channel_id=1, replica_groups=mesh['dp'=4,'node'=4,'local'=2] {'node','local'}, dimensions={0}, use_global_device_ids=true | all-gather | bytes 288 | tf_op jit(solution)/shard_map/all_gather | solution.py:73
  17.8 0.1 copy.53
  17.9 0.1 copy.48
  18.0 1.3 fusion.30
  19.3 0.7 multiply_bitcast_fusion
  20.0 8.7 %all-gather.3 = s32[8,4,2]{1,2,0:T(2,128)S(1)} all-gather(s32[1,4,2]{1,2,0:T(2,128)S(1)} %multiply_bitcast_fusion), channel_id=1, replica_groups=mesh['dp'=4,'node'=4,'local'=2] {'node','local'}, dimensions={0}, use_global_device_ids=true | all-gather | bytes 288 | tf_op jit(solution)/shard_map/all_gather | solution.py:74
  28.8 0.1 copy.55
  28.9 0.1 copy.56
  28.9 0.1 reshape.160
  29.0 0.1 copy.54
  29.1 0.1 reshape.158
  29.2 0.1 eq.41
  29.3 0.1 fusion.15
  29.4 0.1 reduce_window_sum.11
  29.5 0.2 select_reduce_fusion.1
  29.7 0.1 reduce_sum.21
  29.8 0.1 copy.49
  29.9 8.5 %all-gather.5 = bf16[8,4,3584]{2,1,0:T(4,128)(2,1)S(1)} all-gather(bf16[1,4,3584]{2,1,0:T(4,128)(2,1)} %bitcast.46), channel_id=1, replica_groups=mesh['dp'=4,'node'=4,'local'=2] {'node','local'}, dimensions={0}, use_global_device_ids=true | all-gather | bytes 258048 | tf_op jit(solution)/shard_map/all_gather | solution.py:70
  38.4 0.1 reshape.154
  38.5 1.3 fusion.26
  39.8 0.1 select_reduce_fusion
  39.9 1.0 convolution_convert_fusion.2
  40.9 0.2 reshape.139
  41.1 1.2 copy.59
  42.3 4.9 %all-to-all-start.2 = ((bf16[8,4,4,3584]{3,2,0,1:T(4,128)(2,1)}), bf16[8,4,4,3584]{3,2,0,1:T(4,128)(2,1)S(1)}, u32[]{:S(2)}, u32[]{:S(2)}) async-start(bf16[8,4,4,3584]{3,2,0,1:T(4,128)(2,1)} %copy.59), calls=%async_computation.3 | async-start | bytes 1835008 | tf_op jit(solution)/shard_map/all_to_all | solution.py:95
  47.2 9.1 %all-gather.4 = bf16[8,4,3584]{2,1,0:T(4,128)(2,1)S(1)} all-gather(bf16[1,4,3584]{2,1,0:T(4,128)(2,1)S(1)} %bitcast.47), channel_id=1, replica_groups=mesh['dp'=4,'node'=4,'local'=2] {'node','local'}, dimensions={0}, use_global_device_ids=true | all-gather | bytes 258048 | tf_op jit(solution)/shard_map/all_gather | solution.py:69
  56.3 0.1 reshape.152
  56.4 0.1 fusion.14
  56.4 1.4 convolution_convert_fusion.4
  57.8 1.8 reshape.135
  59.6 1.2 copy.57
  60.8 9.8 %all-to-all-done.2 = bf16[8,4,4,3584]{3,2,0,1:T(4,128)(2,1)S(1)} async-done(((bf16[8,4,4,3584]{3,2,0,1:T(4,128)(2,1)}), bf16[8,4,4,3584]{3,2,0,1:T(4,128)(2,1)S(1)}, u32[]{:S(2)}, u32[]{:S(2)}) %all-to-all-start.2) | async-done | bytes 917536 | tf_op jit(solution)/shard_map/all_to_all | solution.py:95
  70.7 3.5 %all-to-all-start = ((bf16[8,4,4,3584]{3,2,0,1:T(4,128)(2,1)}), bf16[8,4,4,3584]{3,2,0,1:T(4,128)(2,1)S(1)}, u32[]{:S(2)}, u32[]{:S(2)}) async-start(bf16[8,4,4,3584]{3,2,0,1:T(4,128)(2,1)} %copy.57), calls=%async_computation | async-start | bytes 1835008 | tf_op jit(solution)/shard_map/all_to_all | solution.py:88
  74.2 0.0 reduce-scatter.3.cloned.1.call-start
  74.2 1.3 copy.60
  75.5 1.7 reshape.140
  77.2 19.6 %all-to-all-done = bf16[8,4,4,3584]{3,2,0,1:T(4,128)(2,1)S(1)} async-done(((bf16[8,4,4,3584]{3,2,0,1:T(4,128)(2,1)}), bf16[8,4,4,3584]{3,2,0,1:T(4,128)(2,1)S(1)}, u32[]{:S(2)}, u32[]{:S(2)}) %all-to-all-start) | async-done | bytes 917536 | tf_op jit(solution)/shard_map/all_to_all | solution.py:88
  96.7 1.3 copy.58
  98.0 1.7 reshape.136
  99.7 1.7 fusion.3
  101.4 0.4 fusion.7
  101.8 0.4 multiply_convert_fusion.1
  102.2 0.3 copy-done.1
  102.5 1.3 convolution_convert_fusion.3
  103.8 0.0 reduce-scatter.3.cloned.1.call-update
  103.9 0.0 reduce-scatter.5.cloned.1.call-start
  103.9 0.4 fusion.9
  104.3 0.8 copy-done.3
  105.1 1.3 fusion
  106.4 0.0 reduce-scatter.5.cloned.1.call-update
  106.5 31.1 %reduce-scatter.3.cloned.1.call-done = bf16[16,3584]{1,0:T(8,128)(2,1)} async-done(((bf16[128,3584]{1,0:T(8,128)(2,1)}), bf16[16,3584]{1,0:T(8,128)(2,1)}) %reduce-scatter.3.cloned.1.call-update) | async-done | bytes 114704 | tf_op jit(solution)/shard_map/reduce_scatter | solution.py:113
  137.6 1.6 reshape.137
  139.2 4.6 %all-to-all-start.1 = ((bf16[4,4,3584]{2,1,0:T(4,128)(2,1)}), bf16[4,4,3584]{2,1,0:T(4,128)(2,1)S(1)}, u32[]{:S(2)}, u32[]{:S(2)}) async-start(bf16[4,4,3584]{2,1,0:T(4,128)(2,1)} %reshape.137), calls=%async_computation.2 | async-start | bytes 229376 | tf_op jit(solution)/shard_map/all_to_all | solution.py:40
  143.8 1.3 fusion.1
  145.1 1.3 fusion.2
  146.5 29.8 %reduce-scatter.5.cloned.1.call-done = bf16[16,3584]{1,0:T(8,128)(2,1)} async-done(((bf16[128,3584]{1,0:T(8,128)(2,1)}), bf16[16,3584]{1,0:T(8,128)(2,1)}) %reduce-scatter.5.cloned.1.call-update) | async-done | bytes 114704 | tf_op jit(solution)/shard_map/reduce_scatter | solution.py:124
  176.3 1.6 reshape.141
  177.9 4.6 %all-to-all-start.3 = ((bf16[4,4,3584]{2,1,0:T(4,128)(2,1)}), bf16[4,4,3584]{2,1,0:T(4,128)(2,1)S(1)}, u32[]{:S(2)}, u32[]{:S(2)}) async-start(bf16[4,4,3584]{2,1,0:T(4,128)(2,1)} %reshape.141), calls=%async_computation.5 | async-start | bytes 229376 | tf_op jit(solution)/shard_map/all_to_all | solution.py:40
  182.5 10.6 %all-gather = bf16[32,4,3584]{2,1,0:T(4,128)(2,1)S(1)} all-gather(bf16[4,4,3584]{2,1,0:T(4,128)(2,1)S(1)} %all-to-all-done.1), channel_id=2, replica_groups=mesh['dp'=4,'node'=4,'local'=2] {'node','local'}, dimensions={0}, use_global_device_ids=true | all-gather | bytes 1032192 | tf_op jit(solution)/shard_map/all_gather | solution.py:51
  193.1 0.2 reshape.138
  193.3 11.4 %all-gather.1 = bf16[32,4,3584]{2,1,0:T(4,128)(2,1)} all-gather(bf16[4,4,3584]{2,1,0:T(4,128)(2,1)S(1)} %all-to-all-done.3), channel_id=3, replica_groups=mesh['dp'=4,'node'=4,'local'=2] {'node','local'}, dimensions={0}, use_global_device_ids=true | all-gather | bytes 1032192 | tf_op jit(solution)/shard_map/all_gather | solution.py:51
  204.7 1.7 reshape.142
  206.3 1.1 convolution_convert_fusion.6
  207.4 0.8 convolution_convert_fusion.5
  (13 shorter events, 0.1 us)
Async XLA Ops:
  7.2 94.6 %copy-start = (bf16[1,128,3584]{2,1,0:T(8,128)(2,1)S(1)}, bf16[1,128,3584]{2,1,0:T(8,128)(2,1)}, u32[]{:S(2)}) copy-start(bf16[1,128,3584]{2,1,0:T(8,128)(2,1)} %param.15) | copy-start | bytes 2752516
  41.1 6.1 %copy-start.4 = (bf16[4,3584]{1,0:T(4,128)(2,1)S(1)}, bf16[4,3584]{1,0:T(4,128)(2,1)}, u32[]{:S(2)}) copy-start(bf16[4,3584]{1,0:T(4,128)(2,1)} %param.9) | copy-start | bytes 86020
  42.3 28.3 %all-to-all-start.2 = ((bf16[8,4,4,3584]{3,2,0,1:T(4,128)(2,1)}), bf16[8,4,4,3584]{3,2,0,1:T(4,128)(2,1)S(1)}, u32[]{:S(2)}, u32[]{:S(2)}) async-start(bf16[8,4,4,3584]{3,2,0,1:T(4,128)(2,1)} %copy.59), calls=%async_computation.3 | async-start | bytes 1835008 | tf_op jit(solution)/shard_map/all_to_all | solution.py:95
  70.7 26.1 %all-to-all-start = ((bf16[8,4,4,3584]{3,2,0,1:T(4,128)(2,1)}), bf16[8,4,4,3584]{3,2,0,1:T(4,128)(2,1)S(1)}, u32[]{:S(2)}, u32[]{:S(2)}) async-start(bf16[8,4,4,3584]{3,2,0,1:T(4,128)(2,1)} %copy.57), calls=%async_computation | async-start | bytes 1835008 | tf_op jit(solution)/shard_map/all_to_all | solution.py:88
  74.2 63.4 %reduce-scatter.3.cloned.1.call-start = ((), (), s32[]{:S(2)}) async-start(), calls=%async_computation.6 | async-start | bytes 1032192 | tf_op jit(solution)/shard_map/reduce_scatter | solution.py:113
  99.7 1.7 copy-start.2
  101.3 1.2 copy-start.1
  103.9 72.4 %reduce-scatter.5.cloned.1.call-start = ((), (), s32[]{:S(2)}) async-start(), calls=%async_computation.7 | async-start | bytes 1032192 | tf_op jit(solution)/shard_map/reduce_scatter | solution.py:124
  103.9 1.2 copy-start.3
  139.2 38.7 %all-to-all-start.1 = ((bf16[4,4,3584]{2,1,0:T(4,128)(2,1)}), bf16[4,4,3584]{2,1,0:T(4,128)(2,1)S(1)}, u32[]{:S(2)}, u32[]{:S(2)}) async-start(bf16[4,4,3584]{2,1,0:T(4,128)(2,1)} %reshape.137), calls=%async_computation.2 | async-start | bytes 229376 | tf_op jit(solution)/shard_map/all_to_all | solution.py:40
  177.9 15.4 %all-to-all-start.3 = ((bf16[4,4,3584]{2,1,0:T(4,128)(2,1)}), bf16[4,4,3584]{2,1,0:T(4,128)(2,1)S(1)}, u32[]{:S(2)}, u32[]{:S(2)}) async-start(bf16[4,4,3584]{2,1,0:T(4,128)(2,1)} %reshape.141), calls=%async_computation.5 | async-start | bytes 229376 | tf_op jit(solution)/shard_map/all_to_all | solution.py:40
Sparse Core Ops, SparseCore 0:
  104.0 33.5 reduce-scatter.2
  140.8 35.4 reduce-scatter.4
where the time goes:
time: 216 us; the launch traced here: 215 us
  waiting for transfers between devices  90.4 us (42%)
  blocking collectives  58.9 us (27%)
  local copies, waits for them, and re-layouts  18.9 us (9%)
  starting transfers between devices  17.7 us (8%)
  between operations  14.2 us (7%)
  matrix products  12.5 us (6%)
  other arithmetic  2.54 us (1%)
    reduce_scatter x1, waiting for transfers between devices, body(): lax.psum_scatter(jnp.dot(hidden, down_slice, preferred_element_type=jnp.f...  31.1 us
    reduce_scatter x1, waiting for transfers between devices, body(): lax.psum_scatter((jnp.dot(gate_delta, gate_slice, preferred_element_type=...  29.8 us
    all_gather x2, blocking collectives, settle(): lax.all_gather(returned[None], ('node', 'local'), axis=0, tiled=True)  22 us
    all_to_all x1, waiting for transfers between devices, body(): lax.all_to_all(buffer_x.reshape(rank_count, experts, shares, model_width)...  19.6 us
    all_gather x1, blocking collectives, body(): lax.all_gather(routes, ('node', 'local'), axis=0, tiled=True)  10.6 us
    all_to_all x1, waiting for transfers between devices, body(): lax.all_to_all(buffer_g.reshape(rank_count, experts, shares, model_width)...  9.81 us
    all_to_all x2, starting transfers between devices, send_back(): lax.all_to_all(rows_kept.reshape(experts, shares, model_width), 'dp', spl...  9.21 us
    all_gather x1, blocking collectives, body(): lax.all_gather(tokens, ('node', 'local'), axis=0, tiled=True)  9.07 us
  transfers between devices with their start and end apart: 6, of which 4 were waited for; matrix products, arithmetic and copies ran while one was open for 7% of the time, Pallas kernels for 0%

commit v1 on v0

v1 whole, which is shorter than its diff:
```python
import functools

import jax
import jax.numpy as jnp
from jax import lax
from jax.experimental import pallas as pl
from jax.experimental.pallas import tpu as pltpu
from jax.sharding import PartitionSpec as P

SEQ = 4096
LANES = 128
PIECES = 4
AXES = ("dp", "node", "local")

bf16, f32, i32 = jnp.bfloat16, jnp.float32, jnp.int32


class Flow:
    def __init__(self, buf, first, second, sizes, width, sems):
        self.buf, self.first, self.second = buf, first, second
        self.n1, self.n2 = sizes[first], sizes[second]
        self.i1, self.i2 = lax.axis_index(first), lax.axis_index(second)
        self.core = lax.axis_index("local")
        self.width = width
        self.s1, self.q1, self.s2, self.q2, self.s0, self.q0 = sems[:6]
        self.t1, self.u1, self.t2, self.u2, self.t0, self.u0 = sems[6:]
        self.sent = []

    def push(self, src, dst, send, recv, axis, peer):
        copy = pltpu.make_async_remote_copy(
            src_ref=src, dst_ref=dst, send_sem=send, recv_sem=recv,
            device_id={axis: peer}, device_id_type=pl.DeviceIdType.MESH,
        )
        copy.start()
        self.sent.append(copy)

    def arrive(self, dst, send, recv, axis, peer):
        pltpu.make_async_remote_copy(
            src_ref=dst, dst_ref=dst, send_sem=send, recv_sem=recv,
            device_id={axis: peer}, device_id_type=pl.DeviceIdType.MESH,
        ).wait_recv()

    def drain(self):
        for copy in self.sent:
            copy.wait_send()
        self.sent = []

    def gather_first(self):
        own = self.buf.at[self.core, self.i2, self.i1]
        for k in range(1, self.n1):
            self.push(own, own, self.s1.at[k], self.q1.at[k], self.first, lax.rem(self.i1 + k, self.n1))

    def gather_second(self):
        for k in range(1, self.n1):
            source = lax.rem(self.i1 + self.n1 - k, self.n1)
            self.arrive(self.buf.at[self.core, self.i2, source], self.s1.at[k], self.q1.at[k], self.first, source)
        own = self.buf.at[self.core, self.i2]
        for k in range(1, self.n2):
            self.push(own, own, self.s2.at[k], self.q2.at[k], self.second, lax.rem(self.i2 + k, self.n2))
        self.push(own, own, self.s0.at[0], self.q0.at[0], "local", 1 - self.core)

    def gather_core(self):
        for k in range(1, self.n2):
            source = lax.rem(self.i2 + self.n2 - k, self.n2)
            block = self.buf.at[self.core, source]
            self.arrive(block, self.s2.at[k], self.q2.at[k], self.second, source)
            self.push(block, block, self.s0.at[k], self.q0.at[k], "local", 1 - self.core)

    def gathered(self):
        for k in range(self.n2):
            source = lax.rem(self.i2 + self.n2 - k, self.n2)
            block = self.buf.at[1 - self.core, source]
            self.arrive(block, self.s0.at[k], self.q0.at[k], "local", 1 - self.core)

    def lanes(self, *index):
        return self.buf.at[(*index, Ellipsis, pl.ds(0, self.width))]

    def sum_core(self, r0):
        self.push(self.lanes(1 - self.core), r0, self.t0, self.u0, "local", 1 - self.core)

    def sum_second(self, r0, r1):
        self.arrive(r0, self.t0, self.u0, "local", 1 - self.core)
        for k in list(range(1, self.n2)) + [0]:
            peer = lax.rem(self.i2 + k, self.n2)
            kept = self.lanes(self.core, peer)
            kept[...] = (kept[...].astype(f32) + r0[peer].astype(f32)).astype(bf16)
            if k:
                self.push(kept, r1.at[k - 1], self.t2.at[k], self.u2.at[k], self.second, peer)

    def sum_first(self, r1, r2):
        kept = self.lanes(self.core, self.i2)
        for k in range(1, self.n2):
            source = lax.rem(self.i2 + self.n2 - k, self.n2)
            self.arrive(r1.at[k - 1], self.t2.at[k], self.u2.at[k], self.second, source)
        total = kept[...].astype(f32)
        for k in range(1, self.n2):
            total = total + r1[k - 1].astype(f32)
        kept[...] = total.astype(bf16)
        for k in range(1, self.n1):
            peer = lax.rem(self.i1 + k, self.n1)
            self.push(self.lanes(self.core, self.i2, peer), r2.at[k - 1], self.t1.at[k], self.u1.at[k], self.first, peer)

    def summed(self, r2):
        total = self.lanes(self.core, self.i2, self.i1)[...].astype(f32)
        for k in range(1, self.n1):
            source = lax.rem(self.i1 + self.n1 - k, self.n1)
            self.arrive(r2.at[k - 1], self.t1.at[k], self.u1.at[k], self.first, source)
            total = total + r2[k - 1].astype(f32)
        return total


def kernel(sizes, tok, routes, fix, keep, lens, cot, wg_hbm, wu_hbm, wd_hbm,
           layer_out, token_grad, grad_gate, grad_down,
           buf_a, buf_b, stage, wg, wu, wd, xs, gs, cw, fw, back, hid, gd,
           r0a, r1a, r2a, r0b, r1b, r2b, wsem, *sems):
    nd, nn, nl = (sizes[a] for a in AXES)
    me_d, me_n, me_l = (lax.axis_index(a) for a in AXES)
    rows, width = tok.shape
    topk = routes.shape[1]
    piece = width // PIECES
    ranks = nn * nl
    group = rows * ranks
    chunk = rows * PIECES
    block = ranks * chunk
    span = 2 * SEQ // ranks
    total_rows = nd * group
    a = Flow(buf_a, "dp", "node", sizes, piece, sems[:12])
    b = Flow(buf_b, "node", "dp", sizes, piece, sems[12:])

    loads = [pltpu.make_async_copy(src, dst, wsem.at[k])
             for k, (src, dst) in enumerate(((wg_hbm, wg), (wu_hbm, wu), (wd_hbm, wd)))]
    for load in loads:
        load.start()

    barrier = pltpu.get_barrier_semaphore()
    for axis in AXES:
        for k in range(1, sizes[axis]):
            pl.semaphore_signal(barrier, inc=1, device_id={axis: lax.rem(lax.axis_index(axis) + k, sizes[axis])},
                                device_id_type=pl.DeviceIdType.MESH)

    lane = lax.broadcasted_iota(i32, (rows, LANES), 1)
    number = keep[...] * fix[...]
    high, low = number // 256, lax.rem(number, 256)
    ids = routes[...]
    meta = jnp.zeros((rows, LANES), i32)
    for k in range(topk):
        meta = meta + jnp.where(lane == ids[:, k:k + 1], high[:, k:k + 1], 0)
        meta = meta + jnp.where(lane == ids[:, k:k + 1] + nd, low[:, k:k + 1], 0)
    own_pos = (me_n * nl + me_l) * span + lax.broadcasted_iota(i32, (rows, LANES), 0) * (span // rows)
    both = lens[...]
    length = jnp.where(own_pos // SEQ == 0, both[0:1, 0:1], both[0:1, 1:2])
    meta = meta + jnp.where(lane == 2 * nd, length // 256, 0) + jnp.where(lane == 2 * nd + 1, lax.rem(length, 256), 0)
    stage[...] = jnp.zeros_like(stage)
    stage[0:rows, piece:piece + LANES] = meta.astype(f32)
    for q in range(PIECES):
        stage[q * rows:(q + 1) * rows, 0:piece] = tok[:, q * piece:(q + 1) * piece].astype(f32)
    buf_a[me_l, me_n, me_d] = stage[...].astype(bf16)
    for q in range(PIECES):
        stage[q * rows:(q + 1) * rows, 0:piece] = cot[:, q * piece:(q + 1) * piece].astype(f32)
    buf_b[me_l, me_d, me_n] = stage[:, 0:piece].astype(bf16)

    pl.semaphore_wait(barrier, sum(sizes[axis] - 1 for axis in AXES))
    a.gather_first()
    b.gather_first()

    out_row = lax.broadcasted_iota(i32, (block, block), 0)
    in_row = lax.broadcasted_iota(i32, (block, block), 1)

    def place(wide, tall):
        core, node, part, j = (tall // (nn * chunk), tall // chunk % nn, tall % chunk // rows, tall % rows)
        return wide == part * group + (node * nl + core) * rows + j

    to_rows = place(out_row, in_row).astype(f32).astype(bf16)
    to_chunks = place(in_row, out_row).astype(f32).astype(bf16)
    lane_g = lax.broadcasted_iota(i32, (group, LANES), 1)
    pick_w = jnp.where(lane_g == me_d, 256.0, 0.0) + jnp.where(lane_g == me_d + nd, 1.0, 0.0)
    pick_l = jnp.where(lane_g == 2 * nd, 256.0, 0.0) + jnp.where(lane_g == 2 * nd + 1, 1.0, 0.0)
    member = lax.broadcasted_iota(i32, (group, 1), 0)
    position = member // rows * span + member % rows * (span // rows)
    second = position // SEQ
    inside = (position - second * SEQ).astype(f32)
    sign = (1 - 2 * second).astype(f32)

    def each_group(fn):
        if nd <= 4:
            for g in range(nd):
                fn(g)
        else:
            pl.loop(0, nd)(fn)

    def group_rows(g):
        return pl.ds(g * group if isinstance(g, int) else pl.multiple_of(g * group, group), group)

    def take_x(g):
        got = buf_a[:, :, g].reshape(block, piece + LANES)
        spread = jnp.dot(to_rows, got, preferred_element_type=f32)
        for q in range(PIECES):
            xs[q, group_rows(g), :] = spread[q * group:(q + 1) * group, 0:piece].astype(bf16)
        meta_g = spread[0:group, piece:]
        weight = jnp.sum(meta_g * pick_w, axis=1, keepdims=True) * (1.0 / 65536.0)
        size = jnp.sum(meta_g * pick_l, axis=1, keepdims=True)
        scale = sign * (inside < size).astype(f32) * float(SEQ) / size
        cw[group_rows(g), :] = weight
        fw[group_rows(g), :] = weight * scale

    def take_g(g):
        spread = jnp.dot(to_rows, buf_b[:, g].reshape(block, piece), preferred_element_type=f32)
        factor = fw[group_rows(g), :]
        for q in range(PIECES):
            gs[q, group_rows(g), :] = (spread[q * group:(q + 1) * group, :] * factor).astype(bf16)

    nt = (((1,), (1,)), ((), ()))
    step = min(total_rows, 128)

    def each_block(fn):
        if total_rows == step:
            fn(pl.ds(0, step))
        else:
            pl.loop(0, total_rows // step)(lambda i: fn(pl.ds(pl.multiple_of(i * step, step), step)))

    def project(rows_ref, w_ref, part):
        total = None
        for q in range(PIECES):
            term = lax.dot_general(rows_ref[q, part, :], w_ref[:, q * piece:(q + 1) * piece], nt, preferred_element_type=f32)
            total = term if total is None else total + term
        return total

    def store_back(buf_write):
        def put(g):
            rows_g = jnp.concatenate([back[q, group_rows(g), :] for q in range(PIECES)], axis=0)
            chunks = jnp.dot(to_chunks, rows_g, preferred_element_type=f32).astype(bf16)
            buf_write(g, chunks.reshape(nl, nn, chunk, piece))
        each_group(put)

    gate_s, up_s, sig_s = hid

    def forward(part):
        gate = project(xs, wg, part)
        up = project(xs, wu, part)
        sig = jax.nn.sigmoid(gate)
        gate_s[part, :], up_s[part, :], sig_s[part, :] = gate, up, sig
        hidden = (gate * sig * up).astype(bf16)
        gd[2, part, :] = hidden
        weight = cw[part, :]
        for q in range(PIECES):
            cols = slice(q * piece, (q + 1) * piece)
            back[q, part, :] = (jnp.dot(hidden, wd[:, cols], preferred_element_type=f32) * weight).astype(bf16)

    def backward(part):
        grad = project(gs, wd, part)
        gate, up, sig = gate_s[part, :], up_s[part, :], sig_s[part, :]
        gate_delta = (grad * up * (sig * (1.0 + gate * (1.0 - sig)))).astype(bf16)
        up_delta = (grad * (gate * sig)).astype(bf16)
        gd[0, part, :] = gate_delta
        for q in range(PIECES):
            cols = slice(q * piece, (q + 1) * piece)
            back[q, part, :] = (jnp.dot(gate_delta, wg[:, cols], preferred_element_type=f32)
                                + jnp.dot(up_delta, wu[:, cols], preferred_element_type=f32)).astype(bf16)

    a.gather_second()
    b.gather_second()
    a.gather_core()
    a.gathered()
    a.drain()
    for load in loads:
        load.wait()
    each_group(take_x)
    each_block(forward)

    def write_a(g, value):
        buf_a[:, :, g, :, 0:piece] = value

    def write_b(g, value):
        buf_b[:, g] = value

    store_back(write_a)
    a.sum_core(r0a)
    b.gather_core()
    b.gathered()
    b.drain()
    each_group(take_g)
    each_block(backward)
    store_back(write_b)
    b.sum_core(r0b)
    a.sum_second(r0a, r1a)
    b.sum_second(r0b, r1b)
    delta_t = gd[0].astype(f32).T.astype(bf16)
    hidden_t = gd[2].astype(f32).T.astype(bf16)
    for q in range(PIECES):
        cols = slice(q * piece, (q + 1) * piece)
        grad_gate[:, cols] = jnp.dot(delta_t, xs[q], preferred_element_type=f32).astype(bf16)
        grad_down[:, cols] = jnp.dot(hidden_t, gs[q], preferred_element_type=f32).astype(bf16)
    a.sum_first(r1a, r2a)
    b.sum_first(r1b, r2b)
    for flow, r2, out in ((a, r2a, layer_out), (b, r2b, token_grad)):
        stage[:, 0:piece] = flow.summed(r2)
        for q in range(PIECES):
            out[:, q * piece:(q + 1) * piece] = stage[q * rows:(q + 1) * rows, 0:piece].astype(bf16)
    a.drain()
    b.drain()


def body(sizes, tokens, routes, gate_fix, keep, seq_lengths, cotangent, w_gate, w_up, w_down):
    rows, width = tokens.shape
    nd, nn, nl = (sizes[a] for a in AXES)
    piece = width // PIECES
    hidden = w_gate.shape[1]
    chunk = rows * PIECES
    total = nd * nn * nl * rows
    dma = pltpu.SemaphoreType.DMA

    def flow_sems(n1, n2):
        return [dma((n1,)), dma((n1,)), dma((n2,)), dma((n2,)), dma((n2,)), dma((n2,)),
                dma((n1,)), dma((n1,)), dma((n2,)), dma((n2,)), dma, dma]

    vmem = pl.BlockSpec(memory_space=pltpu.VMEM)
    hbm = pl.BlockSpec(memory_space=pl.ANY)
    out_shape = (
        jax.ShapeDtypeStruct((rows, width), bf16),
        jax.ShapeDtypeStruct((rows, width), bf16),
        jax.ShapeDtypeStruct((hidden, width), bf16),
        jax.ShapeDtypeStruct((hidden, width), bf16),
    )
    scratch = [
        pltpu.VMEM((nl, nn, nd, chunk, piece + LANES), bf16),
        pltpu.VMEM((nl, nd, nn, chunk, piece), bf16),
        pltpu.VMEM((chunk, piece + LANES), f32),
        pltpu.VMEM((hidden, width), bf16),
        pltpu.VMEM((hidden, width), bf16),
        pltpu.VMEM((hidden, width), bf16),
        pltpu.VMEM((PIECES, total, piece), bf16),
        pltpu.VMEM((PIECES, total, piece), bf16),
        pltpu.VMEM((total, 1), f32),
        pltpu.VMEM((total, 1), f32),
        pltpu.VMEM((PIECES, total, piece), bf16),
        [pltpu.VMEM((total, hidden), f32)] * 3,
        pltpu.VMEM((3, total, hidden), bf16),
        pltpu.VMEM((nn, nd, chunk, piece), bf16),
        pltpu.VMEM((nn - 1, nd, chunk, piece), bf16),
        pltpu.VMEM((nd - 1, chunk, piece), bf16),
        pltpu.VMEM((nd, nn, chunk, piece), bf16),
        pltpu.VMEM((nd - 1, nn, chunk, piece), bf16),
        pltpu.VMEM((nn - 1, chunk, piece), bf16),
        dma((3,)),
        *flow_sems(nd, nn),
        *flow_sems(nn, nd),
    ]
    layer_out, token_grad, grad_gate, grad_down = pl.pallas_call(
        functools.partial(kernel, sizes),
        out_shape=out_shape,
        in_specs=[vmem] * 6 + [hbm] * 3,
        out_specs=(vmem,) * 4,
        scratch_shapes=scratch,
        compiler_params=pltpu.CompilerParams(
            collective_id=0, has_side_effects=True, vmem_limit_bytes=63 * 1024 * 1024
        ),
        name="experts",
    )(tokens, routes, gate_fix, keep, seq_lengths, cotangent, w_gate[0], w_up[0], w_down[0])
    return layer_out, token_grad, grad_gate[None], grad_down[None]


def solution(mesh):
    rows = P(AXES, None)
    weights = P("dp", ("node", "local"), None)
    in_specs = (rows, rows, rows, rows, P("dp", None), rows, weights, weights, weights)
    out_specs = (rows, rows, weights, weights)
    sizes = {axis: mesh.shape[axis] for axis in AXES}
    return jax.shard_map(functools.partial(body, sizes), mesh=mesh, in_specs=in_specs, out_specs=out_specs, check_vma=False)
```

time: 216 us -> 51.2 us (0.24)
  the two profiles are of different devices: /device:TPU:0 before, /device:TPU:8 now
where the time goes in v1:
time: 51.2 us; the launch traced here: 50.8 us
  Pallas kernels  42.3 us (83%)
  local copies, waits for them, and re-layouts  7.84 us (15%)
  between operations  0.66 us (1%)
    pallas_call x1, Pallas kernels, body(): pl.pallas_call(functools.partial(kernel, sizes), out_shape=out_shape, in_...  42.3 us
    unnamed x17, local copies, waits for them, and re-layouts  7.84 us

profile of v1, /device:TPU:8, one launch (start us, length us, event | category | flops | bytes accessed | tf_op | source)
XLA Modules:
  0.0 50.8 jit_solution(9479982603260181134)
XLA Ops:
  0.6 0.0 copy-start.2
  0.6 0.7 %copy-done.2 = s32[4,2]{0,1:T(2,128)S(1)} copy-done((s32[4,2]{0,1:T(2,128)S(1)}, s32[4,2]{0,1:T(2,128)}, u32[]{:S(2)}) %copy-start.2) | copy-done | bytes 56
  1.3 0.0 copy-start.3
  1.3 0.7 %copy.13.routes = s32[4,2]{1,0:T(4,128)} copy(s32[4,2]{0,1:T(2,128)S(1)} %copy-done.2) | data formatting | bytes 64 | tf_op args[1]
  2.0 0.0 copy-done.3
  2.0 0.0 copy-start.4
  2.0 0.7 %copy.14.fix = s32[4,2]{1,0:T(4,128)} copy(s32[4,2]{0,1:T(2,128)S(1)} %copy-done.3) | data formatting | bytes 64 | tf_op args[2]
  2.7 0.0 copy-done.4
  2.7 0.7 %copy.15.keep = s32[4,2]{1,0:T(4,128)} copy(s32[4,2]{0,1:T(2,128)S(1)} %copy-done.4) | data formatting | bytes 64 | tf_op args[3]
  3.3 42.3 %experts.1 = (bf16[4,3584]{1,0:T(4,128)(2,1)}, bf16[4,3584]{1,0:T(4,128)(2,1)}, bf16[128,3584]{1,0:T(8,128)(2,1)}, bf16[128,3584]{1,0:T(8,128)(2,1)}) custom-call(bf16[4,3584]{1,0:T(4,128)(2,1)} %tok.1, s32[4,2]{1,0:T(4,128)} %copy.13.routes, s32[4,2]{1,0:T(4,128)} %copy.14.fix, s32[4,2]{1,0:T(4,128)} %copy.15.keep, s32[1,2]{1,0:T(1,128)} %lens.1, ...), custom_call_target="tpu_custom_call" | custom-call | tf_op jit(solution)/shard_map/experts/pallas_call | solution.py:348
  45.7 0.0 copy-start.1
  45.7 1.4 %copy.20 = bf16[4,3584]{1,0:T(4,128)(2,1)} copy(bf16[4,3584]{1,0:T(4,128)(2,1)} %get-tuple-element.16) | data formatting | bytes 57344
  47.0 0.0 copy-done.1
  47.0 0.6 %copy.21 = bf16[4,3584]{1,0:T(4,128)(2,1)} copy(bf16[4,3584]{1,0:T(4,128)(2,1)S(1)} %copy-done.1) | data formatting | bytes 57344
  47.7 0.0 copy-start
  47.7 2.2 %copy.22 = bf16[1,128,3584]{2,1,0:T(8,128)(2,1)} copy(bf16[1,128,3584]{2,1,0:T(8,128)(2,1)} %bitcast.6) | data formatting | bytes 1835008
  49.9 0.0 copy-done
  49.9 0.9 %copy.23 = bf16[1,128,3584]{2,1,0:T(8,128)(2,1)} copy(bf16[1,128,3584]{2,1,0:T(8,128)(2,1)S(1)} %bitcast.5) | data formatting | bytes 1835008
Async XLA Ops:
  0.6 0.7 %copy-start.2 = (s32[4,2]{0,1:T(2,128)S(1)}, s32[4,2]{0,1:T(2,128)}, u32[]{:S(2)}) copy-start(s32[4,2]{0,1:T(2,128)} %param.10) | copy-start | bytes 100
  1.3 0.7 %copy-start.3 = (s32[4,2]{0,1:T(2,128)S(1)}, s32[4,2]{0,1:T(2,128)}, u32[]{:S(2)}) copy-start(s32[4,2]{0,1:T(2,128)} %param.11) | copy-start | bytes 100
  2.0 0.7 %copy-start.4 = (s32[4,2]{0,1:T(2,128)S(1)}, s32[4,2]{0,1:T(2,128)}, u32[]{:S(2)}) copy-start(s32[4,2]{0,1:T(2,128)} %param.12) | copy-start | bytes 100
  45.7 1.4 %copy-start.1 = (bf16[4,3584]{1,0:T(4,128)(2,1)S(1)}, bf16[4,3584]{1,0:T(4,128)(2,1)}, u32[]{:S(2)}) copy-start(bf16[4,3584]{1,0:T(4,128)(2,1)} %get-tuple-element.17) | copy-start | bytes 86020
  47.7 2.2 %copy-start = (bf16[128,3584]{1,0:T(8,128)(2,1)S(1)}, bf16[128,3584]{1,0:T(8,128)(2,1)}, u32[]{:S(2)}) copy-start(bf16[128,3584]{1,0:T(8,128)(2,1)} %get-tuple-element.11) | copy-start | bytes 2752516

commit v2 on v1

--- a/solution.py
+++ b/solution.py
@@ -110,13 +110,13 @@
 
 
 def kernel(sizes, tok, routes, fix, keep, lens, cot, wg_hbm, wu_hbm, wd_hbm,
-           layer_out, token_grad, grad_gate, grad_down,
-           buf_a, buf_b, stage, wg, wu, wd, xs, gs, cw, fw, back, hid, gd,
-           r0a, r1a, r2a, r0b, r1b, r2b, wsem, *sems):
+           layer_hbm, token_hbm, gate_hbm, down_hbm, layer_out, token_grad, grad_gate, grad_down,
+           buf_a, buf_c, buf_b, stage, wg, wu, wd, xs, gs, cw, fw, back, hid, gd,
+           r0a, r1a, r2a, r0c, r1c, r2c, r0b, r1b, r2b, wsem, osem, *sems):
     nd, nn, nl = (sizes[a] for a in AXES)
     me_d, me_n, me_l = (lax.axis_index(a) for a in AXES)
     rows, width = tok.shape
-    topk = routes.shape[1]
+    topk = routes.shape[0]
     piece = width // PIECES
     ranks = nn * nl
     group = rows * ranks
@@ -124,8 +124,10 @@
     block = ranks * chunk
     span = 2 * SEQ // ranks
     total_rows = nd * group
+    part_c, part_b = buf_c.shape[-1], buf_b.shape[-1]
     a = Flow(buf_a, "dp", "node", sizes, piece, sems[:12])
-    b = Flow(buf_b, "node", "dp", sizes, piece, sems[12:])
+    c = Flow(buf_c, "dp", "node", sizes, part_c, sems[12:24])
+    b = Flow(buf_b, "node", "dp", sizes, part_b, sems[24:])
 
     loads = [pltpu.make_async_copy(src, dst, wsem.at[k])
              for k, (src, dst) in enumerate(((wg_hbm, wg), (wu_hbm, wu), (wd_hbm, wd)))]
@@ -140,12 +142,16 @@
 
     lane = lax.broadcasted_iota(i32, (rows, LANES), 1)
     number = keep[...] * fix[...]
-    high, low = number // 256, lax.rem(number, 256)
-    ids = routes[...]
+    diagonal = lax.broadcasted_iota(i32, (rows, rows), 0) == lax.broadcasted_iota(i32, (rows, rows), 1)
+
+    def column(values, k):
+        return jnp.sum(jnp.where(diagonal, values[k:k + 1, :], 0), axis=1, keepdims=True)
+
     meta = jnp.zeros((rows, LANES), i32)
     for k in range(topk):
-        meta = meta + jnp.where(lane == ids[:, k:k + 1], high[:, k:k + 1], 0)
-        meta = meta + jnp.where(lane == ids[:, k:k + 1] + nd, low[:, k:k + 1], 0)
+        expert, units = column(routes[...], k), column(number, k)
+        meta = meta + jnp.where(lane == expert, units // 256, 0)
+        meta = meta + jnp.where(lane == expert + nd, lax.rem(units, 256), 0)
     own_pos = (me_n * nl + me_l) * span + lax.broadcasted_iota(i32, (rows, LANES), 0) * (span // rows)
     both = lens[...]
     length = jnp.where(own_pos // SEQ == 0, both[0:1, 0:1], both[0:1, 1:2])
@@ -157,11 +163,13 @@
     buf_a[me_l, me_n, me_d] = stage[...].astype(bf16)
     for q in range(PIECES):
         stage[q * rows:(q + 1) * rows, 0:piece] = cot[:, q * piece:(q + 1) * piece].astype(f32)
-    buf_b[me_l, me_d, me_n] = stage[:, 0:piece].astype(bf16)
+    buf_c[me_l, me_n, me_d] = stage[:, 0:part_c].astype(bf16)
+    buf_b[me_l, me_d, me_n] = stage[:, part_c:piece].astype(bf16)
 
     pl.semaphore_wait(barrier, sum(sizes[axis] - 1 for axis in AXES))
     a.gather_first()
     b.gather_first()
+    c.gather_first()
 
     out_row = lax.broadcasted_iota(i32, (block, block), 0)
     in_row = lax.broadcasted_iota(i32, (block, block), 1)
@@ -204,10 +212,11 @@
         fw[group_rows(g), :] = weight * scale
 
     def take_g(g):
-        spread = jnp.dot(to_rows, buf_b[:, g].reshape(block, piece), preferred_element_type=f32)
         factor = fw[group_rows(g), :]
-        for q in range(PIECES):
-            gs[q, group_rows(g), :] = (spread[q * group:(q + 1) * group, :] * factor).astype(bf16)
+        for got, start, size in ((buf_c[:, :, g], 0, part_c), (buf_b[:, g], part_c, part_b)):
+            spread = jnp.dot(to_rows, got.reshape(block, size), preferred_element_type=f32)
+            for q in range(PIECES):
+                gs[q, group_rows(g), start:start + size] = (spread[q * group:(q + 1) * group, :] * factor).astype(bf16)
 
     nt = (((1,), (1,)), ((), ()))
     step = min(total_rows, 128)
@@ -239,8 +248,10 @@
         up = project(xs, wu, part)
         sig = jax.nn.sigmoid(gate)
         gate_s[part, :], up_s[part, :], sig_s[part, :] = gate, up, sig
-        hidden = (gate * sig * up).astype(bf16)
-        gd[2, part, :] = hidden
+        gd[2, part, :] = (gate * sig * up).astype(bf16)
+
+    def outward(part):
+        hidden = gd[2, part, :]
         weight = cw[part, :]
         for q in range(PIECES):
             cols = slice(q * piece, (q + 1) * piece)
@@ -259,45 +270,74 @@
 
     a.gather_second()
     b.gather_second()
+    c.gather_second()
+    for load in loads:
+        load.wait()
     a.gather_core()
     a.gathered()
-    a.drain()
-    for load in loads:
-        load.wait()
     each_group(take_x)
     each_block(forward)
+    c.gather_core()
+    b.gather_core()
+    each_block(outward)
 
     def write_a(g, value):
         buf_a[:, :, g, :, 0:piece] = value
 
     def write_b(g, value):
-        buf_b[:, g] = value
-
+        buf_c[:, :, g] = value[..., 0:part_c]
+        buf_b[:, g] = value[..., part_c:]
+
+    a.drain()
     store_back(write_a)
     a.sum_core(r0a)
-    b.gather_core()
+    c.gathered()
     b.gathered()
+    each_group(take_g)
+    a.sum_second(r0a, r1a)
+    each_block(backward)
+    c.drain()
     b.drain()
-    each_group(take_g)
-    each_block(backward)
     store_back(write_b)
     b.sum_core(r0b)
-    a.sum_second(r0a, r1a)
+    c.sum_core(r0c)
     b.sum_second(r0b, r1b)
+    c.sum_second(r0c, r1c)
     delta_t = gd[0].astype(f32).T.astype(bf16)
     hidden_t = gd[2].astype(f32).T.astype(bf16)
     for q in range(PIECES):
         cols = slice(q * piece, (q + 1) * piece)
         grad_gate[:, cols] = jnp.dot(delta_t, xs[q], preferred_element_type=f32).astype(bf16)
         grad_down[:, cols] = jnp.dot(hidden_t, gs[q], preferred_element_type=f32).astype(bf16)
+    stores = [pltpu.make_async_copy(src, dst, osem.at[k])
+              for k, (src, dst) in enumerate(((grad_gate, gate_hbm), (grad_down, down_hbm),
+                                              (layer_out, layer_hbm), (token_grad, token_hbm)))]
+    stores[0].start()
+    stores[1].start()
     a.sum_first(r1a, r2a)
     b.sum_first(r1b, r2b)
-    for flow, r2, out in ((a, r2a, layer_out), (b, r2b, token_grad)):
-        stage[:, 0:piece] = flow.summed(r2)
+    c.sum_first(r1c, r2c)
+
+    def finish(out, store):
         for q in range(PIECES):
             out[:, q * piece:(q + 1) * piece] = stage[q * rows:(q + 1) * rows, 0:piece].astype(bf16)
-    a.drain()
-    b.drain()
+        store.start()
+
+    stage[:, 0:piece] = a.summed(r2a)
+    finish(layer_out, stores[2])
+    stage[:, part_c:piece] = b.summed(r2b)
+    stage[:, 0:part_c] = c.summed(r2c)
+    finish(token_grad, stores[3])
+    for flow in (a, b, c):
+        flow.drain()
+    for store in stores:
+        store.wait()
+
+
+def hand_on(*refs):
+    count = len(refs) // 2
+    for src, dst in zip(refs[:count], refs[count:]):
+        dst[...] = src[...]
 
 
 def body(sizes, tokens, routes, gate_fix, keep, seq_lengths, cotangent, w_gate, w_up, w_down):
@@ -306,6 +346,8 @@
     piece = width // PIECES
     hidden = w_gate.shape[1]
     chunk = rows * PIECES
+    part_c = piece // LANES * 4 // 7 * LANES
+    part_b = piece - part_c
     total = nd * nn * nl * rows
     dma = pltpu.SemaphoreType.DMA
 
@@ -322,8 +364,13 @@
         jax.ShapeDtypeStruct((hidden, width), bf16),
     )
     scratch = [
+        pltpu.VMEM((rows, width), bf16),
+        pltpu.VMEM((rows, width), bf16),
+        pltpu.VMEM((hidden, width), bf16),
+        pltpu.VMEM((hidden, width), bf16),
         pltpu.VMEM((nl, nn, nd, chunk, piece + LANES), bf16),
-        pltpu.VMEM((nl, nd, nn, chunk, piece), bf16),
+        pltpu.VMEM((nl, nn, nd, chunk, part_c), bf16),
+        pltpu.VMEM((nl, nd, nn, chunk, part_b), bf16),
         pltpu.VMEM((chunk, piece + LANES), f32),
         pltpu.VMEM((hidden, width), bf16),
         pltpu.VMEM((hidden, width), bf16),
@@ -338,24 +385,32 @@
         pltpu.VMEM((nn, nd, chunk, piece), bf16),
         pltpu.VMEM((nn - 1, nd, chunk, piece), bf16),
         pltpu.VMEM((nd - 1, chunk, piece), bf16),
-        pltpu.VMEM((nd, nn, chunk, piece), bf16),
-        pltpu.VMEM((nd - 1, nn, chunk, piece), bf16),
-        pltpu.VMEM((nn - 1, chunk, piece), bf16),
+        pltpu.VMEM((nn, nd, chunk, part_c), bf16),
+        pltpu.VMEM((nn - 1, nd, chunk, part_c), bf16),
+        pltpu.VMEM((nd - 1, chunk, part_c), bf16),
+        pltpu.VMEM((nd, nn, chunk, part_b), bf16),
+        pltpu.VMEM((nd - 1, nn, chunk, part_b), bf16),
+        pltpu.VMEM((nn - 1, chunk, part_b), bf16),
         dma((3,)),
+        dma((4,)),
+        *flow_sems(nd, nn),
         *flow_sems(nd, nn),
         *flow_sems(nn, nd),
     ]
-    layer_out, token_grad, grad_gate, grad_down = pl.pallas_call(
+    results = pl.pallas_call(
         functools.partial(kernel, sizes),
         out_shape=out_shape,
         in_specs=[vmem] * 6 + [hbm] * 3,
-        out_specs=(vmem,) * 4,
+        out_specs=(hbm,) * 4,
         scratch_shapes=scratch,
         compiler_params=pltpu.CompilerParams(
             collective_id=0, has_side_effects=True, vmem_limit_bytes=63 * 1024 * 1024
         ),
         name="experts",
-    )(tokens, routes, gate_fix, keep, seq_lengths, cotangent, w_gate[0], w_up[0], w_down[0])
+    )(tokens, routes.T, gate_fix.T, keep.T, seq_lengths, cotangent, w_gate[0], w_up[0], w_down[0])
+    layer_out, token_grad, grad_gate, grad_down = pl.pallas_call(
+        hand_on, out_shape=out_shape, in_specs=[vmem] * 4, out_specs=(vmem,) * 4, name="hand_on",
+    )(*results)
     return layer_out, token_grad, grad_gate[None], grad_down[None]
 
 

time: 51.2 us -> 41.9 us (0.82)
  the two profiles are of different devices: /device:TPU:8 before, /device:TPU:0 now
where the time goes in v2:
time: 41.9 us; the launch traced here: 41.7 us
  Pallas kernels  41.1 us (98%)
  between operations  0.64 us (2%)
    pallas_call x1, Pallas kernels, body(): pl.pallas_call(functools.partial(kernel, sizes), out_shape=out_shape, in_...  38.3 us
    pallas_call x1, Pallas kernels, body(): pl.pallas_call(hand_on, out_shape=out_shape, in_specs=[vmem] * 4, out_spe...  2.79 us

profile of v2, /device:TPU:0, one launch (start us, length us, event | category | flops | bytes accessed | tf_op | source)
XLA Modules:
  0.0 41.7 jit_solution(13363567649712163799)
XLA Ops:
  0.6 38.3 %experts.1 = (bf16[4,3584]{1,0:T(4,128)(2,1)}, bf16[4,3584]{1,0:T(4,128)(2,1)}, bf16[128,3584]{1,0:T(8,128)(2,1)}, bf16[128,3584]{1,0:T(8,128)(2,1)}) custom-call(bf16[4,3584]{1,0:T(4,128)(2,1)} %tok.1, s32[2,4]{1,0:T(2,128)} %bitcast.11, s32[2,4]{1,0:T(2,128)} %bitcast.12, s32[2,4]{1,0:T(2,128)} %bitcast.13, s32[1,2]{1,0:T(1,128)} %lens.1, ...), custom_call_target="tpu_custom_call" | custom-call | tf_op jit(solution)/shard_map/experts/pallas_call | solution.py:400
  38.9 2.8 %hand_on.1 = (bf16[4,3584]{1,0:T(4,128)(2,1)}, bf16[4,3584]{1,0:T(4,128)(2,1)}, bf16[128,3584]{1,0:T(8,128)(2,1)}, bf16[128,3584]{1,0:T(8,128)(2,1)}) custom-call(bf16[4,3584]{1,0:T(4,128)(2,1)} %get-tuple-element.12.refs_0_, bf16[4,3584]{1,0:T(4,128)(2,1)} %get-tuple-element.13.refs_1_, bf16[128,3584]{1,0:T(8,128)(2,1)} %get-tuple-element.14.refs_2_, ...), custom_call_target="tpu_custom_call" | custom-call | tf_op jit(solution)/shard_map/hand_on/pallas_call | solution.py:411

commit v3 on v2

--- a/solution.py
+++ b/solution.py
@@ -49,21 +49,26 @@
         own = self.buf.at[self.core, self.i2, self.i1]
         for k in range(1, self.n1):
             self.push(own, own, self.s1.at[k], self.q1.at[k], self.first, lax.rem(self.i1 + k, self.n1))
+        self.pass_on(0)
+
+    def pass_on(self, step):
+        chunk = self.buf.at[self.core, self.i2, lax.rem(self.i1 + self.n1 - step, self.n1)]
+        for k in range(1, self.n2):
+            self.push(chunk, chunk, self.s2.at[k, step], self.q2.at[k], self.second, lax.rem(self.i2 + k, self.n2))
 
     def gather_second(self):
         for k in range(1, self.n1):
             source = lax.rem(self.i1 + self.n1 - k, self.n1)
             self.arrive(self.buf.at[self.core, self.i2, source], self.s1.at[k], self.q1.at[k], self.first, source)
+            self.pass_on(k)
         own = self.buf.at[self.core, self.i2]
-        for k in range(1, self.n2):
-            self.push(own, own, self.s2.at[k], self.q2.at[k], self.second, lax.rem(self.i2 + k, self.n2))
         self.push(own, own, self.s0.at[0], self.q0.at[0], "local", 1 - self.core)
 
     def gather_core(self):
         for k in range(1, self.n2):
             source = lax.rem(self.i2 + self.n2 - k, self.n2)
             block = self.buf.at[self.core, source]
-            self.arrive(block, self.s2.at[k], self.q2.at[k], self.second, source)
+            self.arrive(block, self.s2.at[k, 0], self.q2.at[k], self.second, source)
             self.push(block, block, self.s0.at[k], self.q0.at[k], "local", 1 - self.core)
 
     def gathered(self):
@@ -76,29 +81,34 @@
         return self.buf.at[(*index, Ellipsis, pl.ds(0, self.width))]
 
     def sum_core(self, r0):
-        self.push(self.lanes(1 - self.core), r0, self.t0, self.u0, "local", 1 - self.core)
-
-    def sum_second(self, r0, r1):
-        self.arrive(r0, self.t0, self.u0, "local", 1 - self.core)
         for k in list(range(1, self.n2)) + [0]:
             peer = lax.rem(self.i2 + k, self.n2)
+            self.push(self.lanes(1 - self.core, peer), r0.at[peer], self.t0.at[k], self.u0.at[k], "local", 1 - self.core)
+
+    def sum_second(self, r0, r1):
+        for k in list(range(1, self.n2)) + [0]:
+            peer = lax.rem(self.i2 + k, self.n2)
+            self.arrive(r0.at[peer], self.t0.at[k], self.u0.at[k], "local", 1 - self.core)
             kept = self.lanes(self.core, peer)
             kept[...] = (kept[...].astype(f32) + r0[peer].astype(f32)).astype(bf16)
             if k:
-                self.push(kept, r1.at[k - 1], self.t2.at[k], self.u2.at[k], self.second, peer)
+                for j in list(range(1, self.n1)) + [0]:
+                    goal = lax.rem(self.i1 + j, self.n1)
+                    self.push(self.lanes(self.core, peer, goal), r1.at[k - 1, goal],
+                              self.t2.at[k, j], self.u2.at[k, j], self.second, peer)
 
     def sum_first(self, r1, r2):
-        kept = self.lanes(self.core, self.i2)
-        for k in range(1, self.n2):
-            source = lax.rem(self.i2 + self.n2 - k, self.n2)
-            self.arrive(r1.at[k - 1], self.t2.at[k], self.u2.at[k], self.second, source)
-        total = kept[...].astype(f32)
-        for k in range(1, self.n2):
-            total = total + r1[k - 1].astype(f32)
-        kept[...] = total.astype(bf16)
-        for k in range(1, self.n1):
-            peer = lax.rem(self.i1 + k, self.n1)
-            self.push(self.lanes(self.core, self.i2, peer), r2.at[k - 1], self.t1.at[k], self.u1.at[k], self.first, peer)
+        for j in list(range(1, self.n1)) + [0]:
+            goal = lax.rem(self.i1 + j, self.n1)
+            kept = self.lanes(self.core, self.i2, goal)
+            total = kept[...].astype(f32)
+            for k in range(1, self.n2):
+                source = lax.rem(self.i2 + self.n2 - k, self.n2)
+                self.arrive(r1.at[k - 1, goal], self.t2.at[k, j], self.u2.at[k, j], self.second, source)
+                total = total + r1[k - 1, goal].astype(f32)
+            kept[...] = total.astype(bf16)
+            if j:
+                self.push(kept, r2.at[j - 1], self.t1.at[j], self.u1.at[j], self.first, goal)
 
     def summed(self, r2):
         total = self.lanes(self.core, self.i2, self.i1)[...].astype(f32)
@@ -352,8 +362,8 @@
     dma = pltpu.SemaphoreType.DMA
 
     def flow_sems(n1, n2):
-        return [dma((n1,)), dma((n1,)), dma((n2,)), dma((n2,)), dma((n2,)), dma((n2,)),
-                dma((n1,)), dma((n1,)), dma((n2,)), dma((n2,)), dma, dma]
+        return [dma((n1,)), dma((n1,)), dma((n2, n1)), dma((n2,)), dma((n2,)), dma((n2,)),
+                dma((n1,)), dma((n1,)), dma((n2, n1)), dma((n2, n1)), dma((n2,)), dma((n2,))]
 
     vmem = pl.BlockSpec(memory_space=pltpu.VMEM)
     hbm = pl.BlockSpec(memory_space=pl.ANY)

time: 41.9 us -> 40.3 us (0.962)
  Pallas kernels: 41.1 us -> 39.1 us
    pallas_call x1, Pallas kernels: 38.3 us -> 36.3 us  [body(): pl.pallas_call(functools.partial(kernel, sizes), out_shape=out_shape, in_...]
where the time goes in v3:
time: 40.3 us; the launch traced here: 39.7 us
  Pallas kernels  39.1 us (97%)
  between operations  0.64 us (2%)
    pallas_call x1, Pallas kernels, body(): pl.pallas_call(functools.partial(kernel, sizes), out_shape=out_shape, in_...  36.3 us
    pallas_call x1, Pallas kernels, body(): pl.pallas_call(hand_on, out_shape=out_shape, in_specs=[vmem] * 4, out_spe...  2.79 us

profile of v3, /device:TPU:0, one launch (start us, length us, event | category | flops | bytes accessed | tf_op | source)
XLA Modules:
  0.0 39.7 jit_solution(8696741650100620620)
XLA Ops:
  0.6 36.3 %experts.1 = (bf16[4,3584]{1,0:T(4,128)(2,1)}, bf16[4,3584]{1,0:T(4,128)(2,1)}, bf16[128,3584]{1,0:T(8,128)(2,1)}, bf16[128,3584]{1,0:T(8,128)(2,1)}) custom-call(bf16[4,3584]{1,0:T(4,128)(2,1)} %tok.1, s32[2,4]{1,0:T(2,128)} %bitcast.11, s32[2,4]{1,0:T(2,128)} %bitcast.12, s32[2,4]{1,0:T(2,128)} %bitcast.13, s32[1,2]{1,0:T(1,128)} %lens.1, ...), custom_call_target="tpu_custom_call" | custom-call | tf_op jit(solution)/shard_map/experts/pallas_call | solution.py:410
  37.0 2.8 %hand_on.1 = (bf16[4,3584]{1,0:T(4,128)(2,1)}, bf16[4,3584]{1,0:T(4,128)(2,1)}, bf16[128,3584]{1,0:T(8,128)(2,1)}, bf16[128,3584]{1,0:T(8,128)(2,1)}) custom-call(bf16[4,3584]{1,0:T(4,128)(2,1)} %get-tuple-element.12.refs_0_, bf16[4,3584]{1,0:T(4,128)(2,1)} %get-tuple-element.13.refs_1_, bf16[128,3584]{1,0:T(8,128)(2,1)} %get-tuple-element.14.refs_2_, ...), custom_call_target="tpu_custom_call" | custom-call | tf_op jit(solution)/shard_map/hand_on/pallas_call | solution.py:421
